TPU v7x, 32 devices: a whole 2x2x4 slice. The times are simulated.
32 devices in a mesh: dp: 8 (over z, x), mp: 4 (over y, core).
Axes of the slice: x: 2, y: 2, z: 4, core: 2. Of those that a mesh axis runs over, the one named last changes fastest.
Arguments:
- states: bfloat16 [65536, 2048], P(('dp', 'mp')), may hold values from -6 to 6
- dest_device: int32 [65536, 1], P(('dp', 'mp')), may hold values from 0 to 7; in each aligned block of 2048 rows (0 to 2047, 2048 to 4095, ...) at most 320 rows name the same one
- goals: bfloat16 [81920, 1024], P(('dp', 'mp')), may hold values from -6 to 6
- returns: bfloat16 [81920], P(('dp', 'mp')), may hold values from -9 to 9
- weight_in: bfloat16 [3072, 512], P('mp'), may hold values from -0.109375 to 0.109375
- weight_hidden: bfloat16 [3, 512, 512], P(None, 'mp'), may hold values from -0.25 to 0.25
- norm_gain: bfloat16 [4, 512], P(None, 'mp'), may hold values from 0.5 to 1.5
- norm_shift: bfloat16 [4, 512], P(None, 'mp'), may hold values from -1.5 to 1.5
- weight_out: bfloat16 [512], P('mp'), may hold values from -0.25 to 0.25
Outputs:
- total_loss: float32 [], replicated
- grad_states: bfloat16 [65536, 2048], P(('dp', 'mp'))
- grad_goals: bfloat16 [81920, 1024], P(('dp', 'mp'))
- grad_weight_in: float32 [3072, 512], P(None, ('dp', 'mp'))
- grad_weight_hidden: float32 [3, 512, 512], P(None, None, ('dp', 'mp'))
- grad_norm_gain: float32 [4, 512], P(None, ('dp', 'mp'))
- grad_norm_shift: float32 [4, 512], P(None, ('dp', 'mp'))
- grad_weight_out: float32 [512], P(('dp', 'mp'))
Inputs may be any that keep to these rules, and one draw needn't show every extreme that they name: `dest_device`: the 2048 rows of one device name each destination at most 320 times, a bound that some block reaches.
All inputs are finite; a program needn't handle non-finite values.
Results may differ from a plain program's by a relative error of at most 0.019.
Values may be sent and summed in bfloat16 or wider, within the bound.
No kernel may reach another device: no remote copies, remote signals or barrier semaphores. Data moves between devices by JAX's collectives and lax.ppermute only.
A program may use at most 192 MiB of HBM per device.

v0:
```python
import jax
import jax.numpy as jnp
from jax import lax
from jax.sharding import PartitionSpec as P


def norm_act(values, gain, shift):
    center = values - jnp.mean(values, axis=-1, keepdims=True)
    spread = jnp.mean(center * center, axis=-1, keepdims=True)
    return jax.nn.elu(center * lax.rsqrt(spread + 1e-05) * gain + shift)


def left_product(first, second):
    return lax.dot_general(
        first, second, (((0,), (0,)), ((), ())), preferred_element_type=jnp.float32
    )


def right_product(first, second):
    return lax.dot_general(
        first, second, (((1,), (1,)), ((), ())), preferred_element_type=jnp.float32
    )


def shards(
    states, dest_device, goals, returns, weight_in, weight_hidden, norm_gain, norm_shift, weight_out
):
    dp_count = lax.axis_size("dp")
    all_rows = states.shape[0] * dp_count * lax.axis_size("mp")
    slot_count = returns.shape[0]
    capacity = slot_count // dp_count
    feat_width = states.shape[1]
    layer_count = norm_gain.shape[0]
    full_in, full_hidden, full_gain, full_shift, full_out = (
        lax.all_gather(weight_in, "mp", axis=0, tiled=True),
        lax.all_gather(weight_hidden, "mp", axis=1, tiled=True),
        lax.all_gather(norm_gain, "mp", axis=1, tiled=True),
        lax.all_gather(norm_shift, "mp", axis=1, tiled=True),
        lax.all_gather(weight_out, "mp", axis=0, tiled=True),
    )
    dest_index = dest_device[:, 0]
    dest_onehot = (dest_index[:, None] == jnp.arange(dp_count, dtype=jnp.int32)[None, :]).astype(
        jnp.int32
    )
    rank_within = jnp.sum((jnp.cumsum(dest_onehot, axis=0) - dest_onehot) * dest_onehot, axis=1)
    slot_index = dest_index * capacity + rank_within
    send_states = jnp.zeros((slot_count, feat_width), jnp.bfloat16).at[slot_index].set(states)
    send_marks = (
        jnp.zeros((slot_count,), jnp.bfloat16)
        .at[slot_index]
        .set(jnp.ones_like(dest_index, jnp.bfloat16))
    )
    got_states, got_marks = (
        lax.all_to_all(
            send_states.reshape(dp_count, capacity, feat_width),
            "dp",
            split_axis=0,
            concat_axis=0,
            tiled=True,
        ),
        lax.all_to_all(
            send_marks.reshape(dp_count, capacity), "dp", split_axis=0, concat_axis=0, tiled=True
        ),
    )
    row_states = got_states.reshape(slot_count, feat_width)
    valid_mask = got_marks.reshape(slot_count).astype(jnp.float32)
    return_values = returns.astype(jnp.float32)
    local_square = jnp.sum(valid_mask * return_values * return_values)
    square_total = lax.psum(local_square, ("dp", "mp"))
    scale_value = jnp.sqrt(square_total / all_rows + 1e-06)
    inputs = jnp.concatenate([row_states, goals], axis=1)
    layer_inputs = [inputs]
    pullbacks = []
    hidden = inputs
    for layer_number in range(layer_count):
        matrix = full_in if layer_number == 0 else full_hidden[layer_number - 1]
        projected = jnp.dot(hidden, matrix, preferred_element_type=jnp.float32)
        activated, pullback = jax.vjp(
            norm_act,
            projected,
            full_gain[layer_number].astype(jnp.float32),
            full_shift[layer_number].astype(jnp.float32),
        )
        hidden = activated.astype(jnp.bfloat16)
        pullbacks.append(pullback)
        layer_inputs.append(hidden)
    value_pred = jnp.dot(hidden, full_out, preferred_element_type=jnp.float32)
    row_error = valid_mask * (value_pred - return_values / scale_value)
    total_loss = lax.psum(0.5 * jnp.sum(row_error * row_error) / all_rows, ("dp", "mp"))
    grad_value = (row_error / all_rows).astype(jnp.bfloat16)
    grad_out = jnp.dot(grad_value, hidden, preferred_element_type=jnp.float32)
    grad_hidden = grad_value.astype(jnp.float32)[:, None] * full_out.astype(jnp.float32)[None, :]
    hidden_grads = [None] * (layer_count - 1)
    gain_grads = [None] * layer_count
    shift_grads = [None] * layer_count
    grad_in = None
    for layer_number in reversed(range(layer_count)):
        grad_pre, grad_gain, grad_shift = pullbacks[layer_number](grad_hidden)
        grad_pre = grad_pre.astype(jnp.bfloat16)
        gain_grads[layer_number] = grad_gain
        shift_grads[layer_number] = grad_shift
        matrix = full_in if layer_number == 0 else full_hidden[layer_number - 1]
        weight_grad = left_product(layer_inputs[layer_number], grad_pre)
        if layer_number > 0:
            hidden_grads[layer_number - 1] = weight_grad
        else:
            grad_in = weight_grad
        grad_hidden = right_product(grad_pre, matrix)
    grad_state_rows = grad_hidden[:, :feat_width].astype(jnp.bfloat16)
    grad_goal_rows = grad_hidden[:, feat_width:].astype(jnp.bfloat16)
    came_back = lax.all_to_all(
        grad_state_rows.reshape(dp_count, capacity, feat_width),
        "dp",
        split_axis=0,
        concat_axis=0,
        tiled=True,
    )
    grad_states = came_back.reshape(slot_count, feat_width)[slot_index]
    shares = (
        lax.psum_scatter(grad_in, ("dp", "mp"), scatter_dimension=1, tiled=True),
        lax.psum_scatter(jnp.stack(hidden_grads), ("dp", "mp"), scatter_dimension=2, tiled=True),
        lax.psum_scatter(jnp.stack(gain_grads), ("dp", "mp"), scatter_dimension=1, tiled=True),
        lax.psum_scatter(jnp.stack(shift_grads), ("dp", "mp"), scatter_dimension=1, tiled=True),
        lax.psum_scatter(grad_out, ("dp", "mp"), scatter_dimension=0, tiled=True),
    )
    return (
        total_loss,
        grad_states,
        grad_goal_rows,
        shares[0],
        shares[1],
        shares[2],
        shares[3],
        shares[4],
    )


def solution(mesh):
    placed = (
        P(("dp", "mp"), None),
        P(("dp", "mp"), None),
        P(("dp", "mp"), None),
        P(("dp", "mp")),
        P("mp", None),
        P(None, "mp", None),
        P(None, "mp"),
        P(None, "mp"),
        P("mp"),
    )
    return jax.shard_map(
        shards,
        mesh=mesh,
        in_specs=placed,
        out_specs=(
            P(),
            P(("dp", "mp"), None),
            P(("dp", "mp"), None),
            P(None, ("dp", "mp")),
            P(None, None, ("dp", "mp")),
            P(None, ("dp", "mp")),
            P(None, ("dp", "mp")),
            P(("dp", "mp")),
        ),
        check_vma=False,
    )
```

profile of v0, /device:TPU:0, one launch (start us, length us, event | category | flops | bytes accessed | tf_op | source)
XLA Modules:
  0.0 1056.7 jit_solution(1476735436434677186)
XLA Ops:
  7.2 0.7 fusion.23
  7.9 2.3 reduce-window.6
  10.7 0.7 fusion.22
  11.4 0.7 compare_select_fusion.8
  12.2 14.6 %scatter_custom_fusion = bf16[2560]{0:T(1024)(128)(2,1)S(1)} fusion(s32[2048]{0:T(1024)S(1)} %bitcast.104, bf16[2048]{0:T(1024)(128)(2,1)S(1)} %broadcast.175, bf16[]{:T(256)} %constant.61.clone.1), kind=kCustom, calls=%fused_computation.111 | custom fusion | bytes 5122 | tf_op jit(solution)/shard_map/scatter | solution.py:51
  26.9 0.5 broadcast.232
  27.4 0.7 reduce.7
  28.1 0.7 reshape.256
  28.7 7.3 all-to-all-start
  36.0 19.2 %scatter_custom_fusion.1 = bf16[2560,2048]{1,0:T(8,128)(2,1)} fusion(s32[2048]{0:T(1024)S(1)} %bitcast.105, bf16[2048,2048]{1,0:T(8,128)(2,1)} %param.9, bf16[]{:T(256)} %constant.61.clone.1), kind=kCustom, calls=%fused_computation.54 | custom fusion | bytes 10486272 | tf_op jit(solution)/shard_map/scatter | solution.py:47
  55.2 6.1 all-to-all-start.1
  61.4 0.7 all-gather.4.cloned.1.call-update
  62.1 0.7 all-gather.6.cloned.1.call-update
  62.9 5.0 all-gather
  67.9 5.1 all_gather.16
  73.0 5.1 all_gather.17
  78.3 0.6 fusion.26
  78.9 230.2 %psum.14 = f32[]{:T(128)} all-reduce(f32[]{:T(128)} %fusion.26), channel_id=1, replica_groups=mesh['dp'=8,'mp'=4] {'dp','mp'}, use_global_device_ids=true, to_apply=%region_14.15 | all-reduce | flops 1 | bytes 8 | tf_op jit(solution)/shard_map/psum | solution.py:69
  309.8 14.5 %fusion.48 = (f32[2560]{0:T(1024)S(1)}, f32[2560,512]{0,1:T(8,128)}) fusion(bf16[3072,512]{1,0:T(8,128)(2,1)} %all-gather.4.cloned.1.call-done, bf16[2560,1024]{1,0:T(8,128)(2,1)} %param.11, bf16[2560,2048]{1,0:T(8,128)(2,1)} %bitcast.6), kind=kOutput, calls=%fused_computation.132 | convolution fusion | flops 8085829120 | bytes 24127488 | tf_op jit(solution)/shard_map/dot_general | solution.py:77
  324.4 3.1 multiply_reduce_fusion.11
  327.5 6.2 fusion.49
  333.7 0.6 multiply_reduce_fusion.10
  334.4 1.9 copy-done.11
  336.3 3.7 fusion.50
  339.9 0.7 multiply_reduce_fusion.9
  340.6 4.1 fusion.51
  344.7 0.7 multiply_reduce_fusion.8
  345.4 3.0 fusion.5
  348.3 0.4 convolution_reduce_fusion
  348.8 0.6 fusion.47
  349.4 4.6 fusion.42
  354.0 4.0 fusion.46
  358.0 6.3 multiply_reduce_fusion.1
  364.4 6.5 fusion.45
  370.8 8.6 multiply_reduce_fusion.2
  379.4 4.0 fusion.44
  383.5 4.3 multiply_reduce_fusion.3
  387.8 1.5 fusion.43
  389.4 2.3 copy-done.2
  391.6 13.9 %convolution_convert_fusion = bf16[2560,3072]{1,0:T(8,128)(2,1)} fusion(bf16[3072,512]{1,0:T(8,128)(2,1)} %all-gather.4.cloned.1.call-done, f32[2560,512]{0,1:T(8,128)S(1)} %get-tuple-element.47, f32[2560]{0:T(1024)S(1)} %negate_multiply_fusion), kind=kOutput, calls=%fused_computation.3 | convolution fusion | flops 8063549440 | bytes 24127488 | tf_op jit(solution)/shard_map/dot_general | solution.py:20
  405.6 10.2 slice.79
  415.7 5.3 all-to-all-start.2
  421.1 0.9 copy.45
  422.1 0.9 copy.43
  423.1 7.3 convolution_bitcast_fusion
  430.4 7.3 convolution_bitcast_fusion.1
  437.7 3.1 convolution_bitcast_fusion.2
  440.9 2.0 pad_maximum_fusion.3
  442.8 5.1 copy.38
  448.0 0.3 reduce-scatter.8.cloned.1.call-start
  448.3 15.0 %fusion = f32[3072,512]{0,1:T(8,128)} fusion(bf16[2560,1024]{1,0:T(8,128)(2,1)} %param.11, bf16[2560,2048]{1,0:T(8,128)(2,1)} %bitcast.6, f32[2560,512]{0,1:T(8,128)} %copy-done.2, f32[2560]{0:T(1024)S(1)} %negate_multiply_fusion), kind=kOutput, calls=%fused_computation.5 | convolution fusion | flops 8087142400 | bytes 27273216 | tf_op jit(solution)/shard_map/dot_general | solution.py:14
  463.3 0.7 copy-done.6
  464.6 0.8 fusion.52
  465.4 205.4 %all-reduce.2 = (f32[]{:T(128)}, f32[512]{0:T(512)S(1)}) all-reduce(f32[]{:T(128)S(6)} %div.101, f32[512]{0:T(512)S(1)} %bitcast.116), channel_id=1, replica_groups=mesh['dp'=8,'mp'=4] {'dp','mp'}, use_global_device_ids=true, to_apply=%region_16.17 | all-reduce | flops 513 | bytes 4104 | tf_op jit(solution)/shard_map/psum | solution.py:89
  670.8 5.4 slice.80
  676.2 0.6 dynamic-slice.1
  676.8 1.3 copy.46
  678.2 108.3 %reduce-scatter.10.cloned.1.call-done = f32[16,4]{1,0:T(8,128)} async-done(((f32[512,4]{1,0:T(8,128)}), f32[16,4]{1,0:T(8,128)}) %reduce-scatter.10.cloned.1.call-update) | async-done | bytes 272
  786.4 1.3 copy.44
  787.8 142.3 %all-reduce.5.cloned.1.call-done = f32[3,512,512]{1,0,2:T(4,128)} async-done(((f32[3,512,512]{1,0,2:T(4,128)}), f32[3,512,512]{1,0,2:T(4,128)}) %all-reduce.5.cloned.1.call-update) | async-done | bytes 3145744
  930.1 0.9 constant_dynamic-slice_fusion
  931.0 0.7 copy.39
  931.7 21.6 %gather_fusion = bf16[2048,2048]{1,0:T(8,128)(2,1)} fusion(bf16[2560,2048]{1,0:T(8,128)(2,1)} %bitcast.20, s32[2048]{0:T(1024)S(1)} %broadcast_clamp_fusion), kind=kCustom, calls=%fused_computation | custom fusion | bytes 16785408 | tf_op jit(solution)/shard_map/gather | solution.py:118
  953.3 96.1 %reduce-scatter.8.cloned.1.call-done = f32[3072,16]{0,1:T(8,128)} async-done(((f32[3072,512]{0,1:T(8,128)}), f32[3072,16]{0,1:T(8,128)}) %reduce-scatter.8.cloned.1.call-update) | async-done | bytes 196624 | tf_op jit(solution)/shard_map/reduce_scatter | solution.py:120
  (83 shorter events, 1.4 us)
Async XLA Ops:
  12.2 43.0 %copy-start.5 = (s32[2048,1]{0,1:T(1,128)}, s32[2048,1]{0,1:T(1,128)S(1)}, u32[]{:S(2)}) copy-start(s32[2048,1]{0,1:T(1,128)S(1)} %compare_select_fusion.8) | copy-start | bytes 24580
  28.7 26.4 %all-to-all-start = ((bf16[8,2,160]{2,1,0:T(2,128)(2,1)}), bf16[8,2,160]{2,1,0:T(2,128)(2,1)S(1)}, u32[]{:S(2)}, u32[]{:S(2)}) async-start(bf16[8,2,160]{2,1,0:T(2,128)(2,1)} %reshape.256), calls=%async_computation | async-start | bytes 16384 | tf_op jit(solution)/shard_map/all_to_all | solution.py:61
  55.2 7.7 copy-start.10
  55.2 12.7 %copy-start.8 = (bf16[4,128]{1,0:T(4,128)(2,1)S(1)}, bf16[4,128]{1,0:T(4,128)(2,1)}, u32[]{:S(2)}) copy-start(bf16[4,128]{1,0:T(4,128)(2,1)} %param.15) | copy-start | bytes 3076
  55.2 17.8 %copy-start.9 = (bf16[4,128]{1,0:T(4,128)(2,1)S(1)}, bf16[4,128]{1,0:T(4,128)(2,1)}, u32[]{:S(2)}) copy-start(bf16[4,128]{1,0:T(4,128)(2,1)} %param.16) | copy-start | bytes 3076
  55.2 23.1 %copy-start.7 = (bf16[2560]{0:T(1024)(128)(2,1)S(1)}, bf16[2560]{0:T(1024)(128)(2,1)}, u32[]{:S(2)}) copy-start(bf16[2560]{0:T(1024)(128)(2,1)} %param.12) | copy-start | bytes 15364
  55.2 254.6 %all-to-all-start.1 = ((bf16[8,320,2048]{2,1,0:T(8,128)(2,1)}), bf16[8,320,2048]{2,1,0:T(8,128)(2,1)}, u32[]{:S(2)}, u32[]{:S(2)}) async-start(bf16[8,320,2048]{2,1,0:T(8,128)(2,1)} %bitcast.92), calls=%async_computation.1 | async-start | bytes 20971520 | tf_op jit(solution)/shard_map/all_to_all | solution.py:54
  61.4 248.5 %all-gather.4.cloned.1.call-start = ((), (), s32[]{:S(2)}) async-start(), calls=%async_computation.6 | async-start | bytes 3932160 | tf_op jit(solution)/shard_map/all_gather | solution.py:35
  62.1 265.4 %all-gather.6.cloned.1.call-start = ((), (), s32[]{:S(2)}) async-start(), calls=%async_computation.7 | async-start | bytes 1966080 | tf_op jit(solution)/shard_map/all_gather | solution.py:36
  333.7 45.8 %copy-start = (f32[2560,512]{0,1:T(8,128)}, f32[2560,512]{0,1:T(8,128)S(1)}, u32[]{:S(2)}) copy-start(f32[2560,512]{0,1:T(8,128)S(1)} %get-tuple-element.68) | copy-start | bytes 15728644
  333.7 2.6 copy-start.11
  339.9 24.4 %copy-start.1 = (f32[2560,512]{0,1:T(8,128)}, f32[2560,512]{0,1:T(8,128)S(1)}, u32[]{:S(2)}) copy-start(f32[2560,512]{0,1:T(8,128)S(1)} %get-tuple-element.70) | copy-start | bytes 15728644
  358.0 6.3 copy-start.4
  364.3 19.1 %slice-start = ((s8[5242880]{0:T(1024)(128)(4,1)}), s8[4194304]{0:T(1024)(128)(4,1)S(1)}, s32[]{:S(2)}) async-start(s8[5242880]{0:T(1024)(128)(4,1)} %bitcast.93), calls=%async_computation.12 | async-start | bytes 8388608
  370.8 12.6 %slice-start.1 = ((s8[5242880]{0:T(1024)(128)(4,1)}), s8[1048576]{0:T(1024)(128)(4,1)S(1)}, s32[]{:S(2)}) async-start(s8[5242880]{0:T(1024)(128)(4,1)} %bitcast.93), calls=%async_computation.13 | async-start | bytes 2097152
  383.4 4.4 copy-start.3
  389.3 2.3 copy-start.2
  415.7 516.0 %all-to-all-start.2 = ((bf16[8,320,2048]{2,1,0:T(8,128)(2,1)}), bf16[8,320,2048]{2,1,0:T(8,128)(2,1)}, u32[]{:S(2)}, u32[]{:S(2)}) async-start(bf16[8,320,2048]{2,1,0:T(8,128)(2,1)} %bitcast.91), calls=%async_computation.2 | async-start | bytes 20971520 | tf_op jit(solution)/shard_map/all_to_all | solution.py:111
  421.1 255.8 %reduce-scatter.12.cloned.1.call-start = ((), (), s32[]{:S(2)}) async-start(), calls=%async_computation.10 | async-start | bytes 270336
  422.0 364.4 %reduce-scatter.10.cloned.1.call-start = ((), (), s32[]{:S(2)}) async-start(), calls=%async_computation.9 | async-start | bytes 270336
  423.0 507.1 %all-reduce.5.cloned.1.call-start = ((), (), s32[]{:S(2)}) async-start(), calls=%async_computation.11 | async-start | bytes 8388608
  423.1 14.6 %slice-start.2 = ((s8[5242880]{0:T(1024)(128)(4,1)}), s8[4194304]{0:T(1024)(128)(4,1)S(1)}, s32[]{:S(2)}) async-start(s8[5242880]{0:T(1024)(128)(4,1)} %bitcast.95), calls=%async_computation.14 | async-start | bytes 8388608
  423.1 14.6 %slice-start.4 = ((s8[5242880]{0:T(1024)(128)(4,1)}), s8[4194304]{0:T(1024)(128)(4,1)S(1)}, s32[]{:S(2)}) async-start(s8[5242880]{0:T(1024)(128)(4,1)} %bitcast.97), calls=%async_computation.16 | async-start | bytes 8388608
  430.4 7.3 slice-start.3
  430.4 7.3 slice-start.5
  448.0 601.4 %reduce-scatter.8.cloned.1.call-start = ((), (), s32[]{:S(2)}) async-start(), calls=%async_computation.8 | async-start | bytes 6488064 | tf_op jit(solution)/shard_map/reduce_scatter | solution.py:120
  463.3 0.7 copy-start.6
Sparse Core Ops, SparseCore 0:
  63.8 30.3 all-gather.3
  95.7 19.6 all-gather.5
  424.1 226.0 reduce-scatter.11
  652.4 133.9 reduce-scatter.9
  792.4 137.6 all-reduce.4
  936.1 113.2 reduce-scatter.7
where the time goes:
time: 1060 us
  blocking collectives  451 us (43%)
  waiting for transfers between devices  348 us (33%)
  matrix products  95.5 us (9%)
  local copies, waits for them, and re-layouts  89.3 us (8%)
  other arithmetic  37.3 us (4%)
  starting transfers between devices  19.2 us (2%)
  between operations  16.4 us (2%)
    unnamed x9, waiting for transfers between devices  252 us
    psum x1, blocking collectives, shards(): square_total = lax.psum(local_square, ('dp', 'mp'))  230 us
    psum x1, blocking collectives, shards(): lax.psum(0.5 * jnp.sum(row_error * row_error) / all_rows, ('dp', 'mp'))  205 us
    reduce_scatter x1, waiting for transfers between devices, shards(): lax.psum_scatter(grad_in, ('dp', 'mp'), scatter_dimension=1, tiled=True)  96.1 us
    dot_general x4, matrix products, right_product(): lax.dot_general(first, second, (((1,), (1,)), ((), ())), preferred_elemen...  33.1 us
    dot_general x4, matrix products, left_product(): lax.dot_general(first, second, (((0,), (0,)), ((), ())), preferred_elemen...  32.8 us
    dot_general x4, matrix products, shards(): projected = jnp.dot(hidden, matrix, preferred_element_type=jnp.float32)  28.5 us
    gather x1, local copies, waits for them, and re-layouts, shards(): grad_states = came_back.reshape(slot_count, feat_width)[slot_index]  21.6 us
  transfers between devices with their start and end apart: 9, of which 3 were waited for; matrix products, arithmetic and copies ran while one was open for 11% of the time, Pallas kernels for 0%

commit v1 on v0

--- a/solution.py
+++ b/solution.py
@@ -86,7 +86,8 @@
         layer_inputs.append(hidden)
     value_pred = jnp.dot(hidden, full_out, preferred_element_type=jnp.float32)
     row_error = valid_mask * (value_pred - return_values / scale_value)
-    total_loss = lax.psum(0.5 * jnp.sum(row_error * row_error) / all_rows, ("dp", "mp"))
+    half = lax.psum(0.5 * jnp.sum(row_error * row_error) / all_rows, "dp")
+    total_loss = lax.psum(half, "mp")
     grad_value = (row_error / all_rows).astype(jnp.bfloat16)
     grad_out = jnp.dot(grad_value, hidden, preferred_element_type=jnp.float32)
     grad_hidden = grad_value.astype(jnp.float32)[:, None] * full_out.astype(jnp.float32)[None, :]

time: 1060 us -> 1070 us (level)
  blocking collectives: 451 us -> 486 us
  waiting for transfers between devices: 348 us -> 316 us
    unnamed x0 -> x1, blocking collectives: none -> 72.4 us
    psum x1 -> x2, blocking collectives: 205 us -> 168 us  [the longest x1 142 us: shards(): half = lax.psum(0.5 * jnp.sum(row_error * row_error) / all_rows, 'dp')]
    unnamed x9, waiting for transfers between devices: 252 us -> 220 us
where the time goes in v1:
time: 1070 us; the launch traced here: 1060 us
  blocking collectives  486 us (45%)
  waiting for transfers between devices  316 us (30%)
  matrix products  95.5 us (9%)
  local copies, waits for them, and re-layouts  89.3 us (8%)
  other arithmetic  37.3 us (3%)
  starting transfers between devices  19.2 us (2%)
  between operations  16.4 us (2%)
    psum x1, blocking collectives, shards(): square_total = lax.psum(local_square, ('dp', 'mp'))  230 us
    unnamed x9, waiting for transfers between devices  220 us
    psum x1, blocking collectives, shards(): half = lax.psum(0.5 * jnp.sum(row_error * row_error) / all_rows, 'dp')  142 us
    reduce_scatter x1, waiting for transfers between devices, shards(): lax.psum_scatter(grad_in, ('dp', 'mp'), scatter_dimension=1, tiled=True)  96.1 us
    unnamed x1, blocking collectives  72.4 us
    dot_general x4, matrix products, right_product(): lax.dot_general(first, second, (((1,), (1,)), ((), ())), preferred_elemen...  33.1 us
    dot_general x4, matrix products, left_product(): lax.dot_general(first, second, (((0,), (0,)), ((), ())), preferred_elemen...  32.8 us
    dot_general x4, matrix products, shards(): projected = jnp.dot(hidden, matrix, preferred_element_type=jnp.float32)  28.5 us
  transfers between devices with their start and end apart: 9, of which 3 were waited for; matrix products, arithmetic and copies ran while one was open for 11% of the time, Pallas kernels for 0%

profile of v1, /device:TPU:0, one launch (start us, length us, event | category | flops | bytes accessed | tf_op | source)
XLA Modules:
  0.0 1059.7 jit_solution(16021899390404381443)
XLA Ops:
  7.2 0.7 fusion.23
  7.9 2.3 reduce-window.6
  10.7 0.7 fusion.22
  11.4 0.7 compare_select_fusion.8
  12.2 14.6 %scatter_custom_fusion = bf16[2560]{0:T(1024)(128)(2,1)S(1)} fusion(s32[2048]{0:T(1024)S(1)} %bitcast.104, bf16[2048]{0:T(1024)(128)(2,1)S(1)} %broadcast.175, bf16[]{:T(256)} %constant.61.clone.1), kind=kCustom, calls=%fused_computation.111 | custom fusion | bytes 5122 | tf_op jit(solution)/shard_map/scatter | solution.py:51
  26.9 0.5 broadcast.232
  27.4 0.7 reduce.7
  28.1 0.7 reshape.256
  28.7 7.3 all-to-all-start
  36.0 19.2 %scatter_custom_fusion.1 = bf16[2560,2048]{1,0:T(8,128)(2,1)} fusion(s32[2048]{0:T(1024)S(1)} %bitcast.105, bf16[2048,2048]{1,0:T(8,128)(2,1)} %param.9, bf16[]{:T(256)} %constant.61.clone.1), kind=kCustom, calls=%fused_computation.54 | custom fusion | bytes 10486272 | tf_op jit(solution)/shard_map/scatter | solution.py:47
  55.2 6.1 all-to-all-start.1
  61.4 0.7 all-gather.4.cloned.1.call-update
  62.1 0.7 all-gather.6.cloned.1.call-update
  62.9 5.0 all-gather
  67.9 5.1 all_gather.16
  73.0 5.1 all_gather.17
  78.3 0.6 fusion.26
  78.9 230.2 %psum.21 = f32[]{:T(128)} all-reduce(f32[]{:T(128)} %fusion.26), channel_id=1, replica_groups=mesh['dp'=8,'mp'=4] {'dp','mp'}, use_global_device_ids=true, to_apply=%region_14.15 | all-reduce | flops 1 | bytes 8 | tf_op jit(solution)/shard_map/psum | solution.py:69
  309.8 14.5 %fusion.48 = (f32[2560]{0:T(1024)S(1)}, f32[2560,512]{0,1:T(8,128)}) fusion(bf16[3072,512]{1,0:T(8,128)(2,1)} %all-gather.4.cloned.1.call-done, bf16[2560,1024]{1,0:T(8,128)(2,1)} %param.11, bf16[2560,2048]{1,0:T(8,128)(2,1)} %bitcast.6), kind=kOutput, calls=%fused_computation.132 | convolution fusion | flops 8085829120 | bytes 24127488 | tf_op jit(solution)/shard_map/dot_general | solution.py:77
  324.4 3.1 multiply_reduce_fusion.11
  327.5 6.2 fusion.49
  333.7 0.6 multiply_reduce_fusion.10
  334.4 1.9 copy-done.11
  336.3 3.7 fusion.50
  339.9 0.7 multiply_reduce_fusion.9
  340.6 4.1 fusion.51
  344.7 0.7 multiply_reduce_fusion.8
  345.4 3.0 fusion.5
  348.8 0.6 fusion.47
  349.4 4.6 fusion.42
  354.0 4.0 fusion.46
  358.0 6.3 multiply_reduce_fusion.1
  364.4 6.5 fusion.45
  370.8 8.6 multiply_reduce_fusion.2
  379.4 4.0 fusion.44
  383.5 4.3 multiply_reduce_fusion.3
  387.8 1.5 fusion.43
  389.4 2.3 copy-done.2
  391.6 13.9 %convolution_convert_fusion = bf16[2560,3072]{1,0:T(8,128)(2,1)} fusion(bf16[3072,512]{1,0:T(8,128)(2,1)} %all-gather.4.cloned.1.call-done, f32[2560,512]{0,1:T(8,128)S(1)} %get-tuple-element.45, f32[2560]{0:T(1024)S(1)} %negate_multiply_fusion), kind=kOutput, calls=%fused_computation.3 | convolution fusion | flops 8063549440 | bytes 24127488 | tf_op jit(solution)/shard_map/dot_general | solution.py:20
  405.6 10.2 slice.79
  415.7 5.3 all-to-all-start.2
  421.1 0.9 copy.45
  422.1 0.9 copy.43
  423.1 7.3 convolution_bitcast_fusion
  430.4 7.3 convolution_bitcast_fusion.1
  437.7 3.1 convolution_bitcast_fusion.2
  440.9 2.0 pad_maximum_fusion.3
  442.8 5.1 copy.38
  448.3 15.0 %fusion = f32[3072,512]{0,1:T(8,128)} fusion(bf16[2560,1024]{1,0:T(8,128)(2,1)} %param.11, bf16[2560,2048]{1,0:T(8,128)(2,1)} %bitcast.6, f32[2560,512]{0,1:T(8,128)} %copy-done.2, f32[2560]{0:T(1024)S(1)} %negate_multiply_fusion), kind=kOutput, calls=%fused_computation.5 | convolution fusion | flops 8087142400 | bytes 27273216 | tf_op jit(solution)/shard_map/dot_general | solution.py:14
  463.3 0.7 copy-done.6
  464.6 141.9 %psum.22 = f32[]{:T(128)} all-reduce(f32[]{:T(128)S(6)} %div.101), channel_id=1, replica_groups=mesh['dp'=8,'mp'=4] {'dp'}, use_global_device_ids=true, to_apply=%region_16.17 | all-reduce | flops 1 | bytes 8 | tf_op jit(solution)/shard_map/psum | solution.py:89
  606.5 26.1 %psum.23 = f32[]{:T(128)} all-reduce(f32[]{:T(128)} %psum.22), channel_id=1, replica_groups=mesh['dp'=8,'mp'=4] {'mp'}, use_global_device_ids=true, to_apply=%region_17.18 | all-reduce | flops 1 | bytes 8 | tf_op jit(solution)/shard_map/psum | solution.py:90
  632.6 5.4 slice.80
  638.0 0.8 fusion.52
  638.8 72.4 %all-reduce.1 = f32[512]{0:T(512)S(1)} all-reduce(f32[512]{0:T(512)S(1)} %bitcast.116), channel_id=6, replica_groups=mesh['dp'=8,'mp'=4] {'dp','mp'}, use_global_device_ids=true, to_apply=%region_38.39.clone | all-reduce | flops 512 | bytes 4096
  711.3 0.6 dynamic-slice.1
  711.8 1.3 copy.46
  713.2 76.3 %reduce-scatter.10.cloned.1.call-done = f32[16,4]{1,0:T(8,128)} async-done(((f32[512,4]{1,0:T(8,128)}), f32[16,4]{1,0:T(8,128)}) %reduce-scatter.10.cloned.1.call-update) | async-done | bytes 272
  789.5 1.3 copy.44
  790.9 142.3 %all-reduce.4.cloned.1.call-done = f32[3,512,512]{1,0,2:T(4,128)} async-done(((f32[3,512,512]{1,0,2:T(4,128)}), f32[3,512,512]{1,0,2:T(4,128)}) %all-reduce.4.cloned.1.call-update) | async-done | bytes 3145744
  933.1 0.9 constant_dynamic-slice_fusion
  934.1 0.7 copy.39
  934.7 21.6 %gather_fusion = bf16[2048,2048]{1,0:T(8,128)(2,1)} fusion(bf16[2560,2048]{1,0:T(8,128)(2,1)} %bitcast.20, s32[2048]{0:T(1024)S(1)} %broadcast_clamp_fusion), kind=kCustom, calls=%fused_computation | custom fusion | bytes 16785408 | tf_op jit(solution)/shard_map/gather | solution.py:119
  956.4 96.1 %reduce-scatter.8.cloned.1.call-done = f32[3072,16]{0,1:T(8,128)} async-done(((f32[3072,512]{0,1:T(8,128)}), f32[3072,16]{0,1:T(8,128)}) %reduce-scatter.8.cloned.1.call-update) | async-done | bytes 196624 | tf_op jit(solution)/shard_map/reduce_scatter | solution.py:121
  (85 shorter events, 2.2 us)
Async XLA Ops:
  12.2 43.0 %copy-start.5 = (s32[2048,1]{0,1:T(1,128)}, s32[2048,1]{0,1:T(1,128)S(1)}, u32[]{:S(2)}) copy-start(s32[2048,1]{0,1:T(1,128)S(1)} %compare_select_fusion.8) | copy-start | bytes 24580
  28.7 26.4 %all-to-all-start = ((bf16[8,2,160]{2,1,0:T(2,128)(2,1)}), bf16[8,2,160]{2,1,0:T(2,128)(2,1)S(1)}, u32[]{:S(2)}, u32[]{:S(2)}) async-start(bf16[8,2,160]{2,1,0:T(2,128)(2,1)} %reshape.256), calls=%async_computation | async-start | bytes 16384 | tf_op jit(solution)/shard_map/all_to_all | solution.py:61
  55.2 7.7 copy-start.10
  55.2 12.7 %copy-start.8 = (bf16[4,128]{1,0:T(4,128)(2,1)S(1)}, bf16[4,128]{1,0:T(4,128)(2,1)}, u32[]{:S(2)}) copy-start(bf16[4,128]{1,0:T(4,128)(2,1)} %param.15) | copy-start | bytes 3076
  55.2 17.8 %copy-start.9 = (bf16[4,128]{1,0:T(4,128)(2,1)S(1)}, bf16[4,128]{1,0:T(4,128)(2,1)}, u32[]{:S(2)}) copy-start(bf16[4,128]{1,0:T(4,128)(2,1)} %param.16) | copy-start | bytes 3076
  55.2 23.1 %copy-start.7 = (bf16[2560]{0:T(1024)(128)(2,1)S(1)}, bf16[2560]{0:T(1024)(128)(2,1)}, u32[]{:S(2)}) copy-start(bf16[2560]{0:T(1024)(128)(2,1)} %param.12) | copy-start | bytes 15364
  55.2 254.6 %all-to-all-start.1 = ((bf16[8,320,2048]{2,1,0:T(8,128)(2,1)}), bf16[8,320,2048]{2,1,0:T(8,128)(2,1)}, u32[]{:S(2)}, u32[]{:S(2)}) async-start(bf16[8,320,2048]{2,1,0:T(8,128)(2,1)} %bitcast.92), calls=%async_computation.1 | async-start | bytes 20971520 | tf_op jit(solution)/shard_map/all_to_all | solution.py:54
  61.4 248.5 %all-gather.4.cloned.1.call-start = ((), (), s32[]{:S(2)}) async-start(), calls=%async_computation.6 | async-start | bytes 3932160 | tf_op jit(solution)/shard_map/all_gather | solution.py:35
  62.1 265.4 %all-gather.6.cloned.1.call-start = ((), (), s32[]{:S(2)}) async-start(), calls=%async_computation.7 | async-start | bytes 1966080 | tf_op jit(solution)/shard_map/all_gather | solution.py:36
  333.7 45.8 %copy-start = (f32[2560,512]{0,1:T(8,128)}, f32[2560,512]{0,1:T(8,128)S(1)}, u32[]{:S(2)}) copy-start(f32[2560,512]{0,1:T(8,128)S(1)} %get-tuple-element.66) | copy-start | bytes 15728644
  333.7 2.6 copy-start.11
  339.9 24.4 %copy-start.1 = (f32[2560,512]{0,1:T(8,128)}, f32[2560,512]{0,1:T(8,128)S(1)}, u32[]{:S(2)}) copy-start(f32[2560,512]{0,1:T(8,128)S(1)} %get-tuple-element.68) | copy-start | bytes 15728644
  358.0 6.3 copy-start.4
  364.3 19.1 %slice-start = ((s8[5242880]{0:T(1024)(128)(4,1)}), s8[4194304]{0:T(1024)(128)(4,1)S(1)}, s32[]{:S(2)}) async-start(s8[5242880]{0:T(1024)(128)(4,1)} %bitcast.93), calls=%async_computation.12 | async-start | bytes 8388608
  370.8 12.6 %slice-start.1 = ((s8[5242880]{0:T(1024)(128)(4,1)}), s8[1048576]{0:T(1024)(128)(4,1)S(1)}, s32[]{:S(2)}) async-start(s8[5242880]{0:T(1024)(128)(4,1)} %bitcast.93), calls=%async_computation.13 | async-start | bytes 2097152
  383.4 4.4 copy-start.3
  389.3 2.3 copy-start.2
  415.7 519.0 %all-to-all-start.2 = ((bf16[8,320,2048]{2,1,0:T(8,128)(2,1)}), bf16[8,320,2048]{2,1,0:T(8,128)(2,1)}, u32[]{:S(2)}, u32[]{:S(2)}) async-start(bf16[8,320,2048]{2,1,0:T(8,128)(2,1)} %bitcast.91), calls=%async_computation.2 | async-start | bytes 20971520 | tf_op jit(solution)/shard_map/all_to_all | solution.py:112
  421.1 290.8 %reduce-scatter.12.cloned.1.call-start = ((), (), s32[]{:S(2)}) async-start(), calls=%async_computation.10 | async-start | bytes 270336
  422.0 367.5 %reduce-scatter.10.cloned.1.call-start = ((), (), s32[]{:S(2)}) async-start(), calls=%async_computation.9 | async-start | bytes 270336
  423.0 510.1 %all-reduce.4.cloned.1.call-start = ((), (), s32[]{:S(2)}) async-start(), calls=%async_computation.11 | async-start | bytes 8388608
  423.1 14.6 %slice-start.2 = ((s8[5242880]{0:T(1024)(128)(4,1)}), s8[4194304]{0:T(1024)(128)(4,1)S(1)}, s32[]{:S(2)}) async-start(s8[5242880]{0:T(1024)(128)(4,1)} %bitcast.95), calls=%async_computation.14 | async-start | bytes 8388608
  423.1 14.6 %slice-start.4 = ((s8[5242880]{0:T(1024)(128)(4,1)}), s8[4194304]{0:T(1024)(128)(4,1)S(1)}, s32[]{:S(2)}) async-start(s8[5242880]{0:T(1024)(128)(4,1)} %bitcast.97), calls=%async_computation.16 | async-start | bytes 8388608
  430.4 7.3 slice-start.3
  430.4 7.3 slice-start.5
  448.0 604.5 %reduce-scatter.8.cloned.1.call-start = ((), (), s32[]{:S(2)}) async-start(), calls=%async_computation.8 | async-start | bytes 6488064 | tf_op jit(solution)/shard_map/reduce_scatter | solution.py:121
  463.3 0.7 copy-start.6
Sparse Core Ops, SparseCore 0:
  63.8 30.3 all-gather.3
  95.7 19.6 all-gather.5
  424.1 232.6 reduce-scatter.11
  659.0 130.5 reduce-scatter.9
  795.5 137.6 all-reduce.3
  939.2 113.2 reduce-scatter.7
